TPU v7x, 32 devices: a whole 2x2x4 slice. The times are simulated.
32 devices in a mesh: grp: 2 (over x), dp: 4 (over y, core), mp: 4 (over z).
Axes of the slice: x: 2, y: 2, z: 4, core: 2. Of those that a mesh axis runs over, the one named last changes fastest.
Arguments:
- queries: bfloat16 [4, 512, 4096], P('dp', None, 'mp'), may hold values from -5 to 5
- keys: bfloat16 [4, 512, 512], P('dp'), may hold values from -5 to 5
- values: bfloat16 [4, 512, 512], P('dp'), may hold values from -6 to 6
- out_weight: bfloat16 [4096, 5120], P('mp'), may hold values from -0.09375 to 0.09375
- residual: bfloat16 [4, 512, 5120], P('dp', 'mp'), may hold values from -24 to 24
- student_hidden: bfloat16 [4, 512, 2560], P('dp', 'mp'), may hold values from -6 to 6
- norm_gain: float32 [2560], replicated, may hold values from 0.5 to 1.5
- projection: bfloat16 [2560, 5120], P(None, ('grp', 'dp')), may hold values from -0.125 to 0.125
- lengths: int32 [4], replicated, may hold values from 128 to 512, as said below
Outputs:
- teacher_out: bfloat16 [4, 512, 5120], P('dp', 'mp', 'grp')
- distill_loss: float32 [], replicated
- grad_proj: float32 [2560, 5120], P('mp', ('grp', 'dp'))
- grad_gain: float32 [2560], P('grp')
- grad_hidden: float32 [4, 512, 2560], P('dp', 'mp', 'grp')
Inputs may be any that keep to these rules, and one draw needn't show every extreme that they name: `lengths`: at least one sequence is live throughout.
All inputs are finite; a program needn't handle non-finite values.
Results may differ from a plain program's by a relative error of at most 0.018.
Values may be sent and summed in bfloat16 or wider, within the bound.
A program may use at most 128 MiB of HBM per device.

v0:
```python
import jax
import jax.numpy as jnp
from jax import lax
from jax.sharding import PartitionSpec as P

D_T = 5120
D_S = 2560
HD = 128
HQ = 32
KVH = 4


def passed_along(array, axis, by):
    length = lax.axis_size(axis)
    pairs = [(i, i + by) for i in range(length) if 0 <= i + by < length]
    return lax.ppermute(array, axis, pairs)


def attend(query_rows, positions, key_rows, value_rows):
    total_rows = query_rows.shape[0]
    block_rows = min(512, total_rows)
    head_count = query_rows.shape[1] // HD
    key_positions = jnp.arange(key_rows.shape[0], dtype=jnp.int32)
    score_scale = HD ** (-0.5)

    def one_block(inputs):
        row_block, row_positions = inputs
        query_heads = row_block.reshape(block_rows, head_count, HD)
        scores = (
            jnp.einsum("bhd,kd->hbk", query_heads, key_rows, preferred_element_type=jnp.float32)
            * score_scale
        )
        allowed = row_positions[None, :, None] >= key_positions[None, None, :]
        scores = jnp.where(allowed, scores, -1e30)
        row_max = jnp.max(scores, axis=-1, keepdims=True)
        exponent = jnp.exp(scores - row_max)
        weights = (exponent / jnp.sum(exponent, axis=-1, keepdims=True)).astype(jnp.bfloat16)
        context_rows = jnp.einsum(
            "hbk,kd->bhd", weights, value_rows, preferred_element_type=jnp.float32
        )
        return context_rows.reshape(block_rows, head_count * HD).astype(jnp.bfloat16)

    blocks = total_rows // block_rows
    result = lax.map(
        one_block,
        (query_rows.reshape(blocks, block_rows, -1), positions.reshape(blocks, block_rows)),
    )
    return result.reshape(total_rows, head_count * HD)


def body(
    queries, keys, values, out_weight, residual, student_hidden, norm_gain, projection, lengths
):
    seq_len = queries.shape[1]
    tok_rows = residual.shape[1]
    half_cols = residual.shape[2] // 2
    grp_index = lax.axis_index("grp")
    mp_index = lax.axis_index("mp")
    local_heads = queries.shape[2] // HD
    kv_head = mp_index * local_heads // (HQ // KVH)
    key_rows = lax.dynamic_slice_in_dim(keys[0], kv_head * HD, HD, 1)
    value_rows = lax.dynamic_slice_in_dim(values[0], kv_head * HD, HD, 1)
    context_width = queries.shape[2]
    out_cols = out_weight.shape[1]
    positions = jnp.arange(seq_len, dtype=jnp.int32)
    context = lax.cond(
        grp_index == 0,
        lambda: attend(queries[0], positions, key_rows, value_rows),
        lambda: jnp.zeros((seq_len, context_width), jnp.bfloat16),
    )
    attn_rows = lax.psum_scatter(
        lax.cond(
            grp_index == 0,
            lambda: jnp.dot(context, out_weight, preferred_element_type=jnp.float32),
            lambda: jnp.zeros((tok_rows * lax.axis_size("mp"), out_cols), jnp.float32),
        ).astype(jnp.bfloat16),
        "mp",
        scatter_dimension=0,
        tiled=True,
    ).astype(jnp.float32)
    full_rows = (residual[0].astype(jnp.float32) + attn_rows).astype(jnp.bfloat16)
    shifted = passed_along(full_rows[:, half_cols:], "grp", 1)
    own_target = jnp.where(grp_index == 0, full_rows[:, :half_cols], shifted)
    hidden = student_hidden[0].astype(jnp.float32)
    inverse_rms = lax.rsqrt(jnp.mean(hidden * hidden, axis=-1, keepdims=True) + 1e-06)
    unit_rows = hidden * inverse_rms
    normed = (unit_rows * norm_gain).astype(jnp.bfloat16)
    normed_all = lax.all_gather(normed, "dp", axis=0, tiled=True)
    targets = lax.all_to_all(own_target, "dp", split_axis=1, concat_axis=0, tiled=True)
    predicted = jnp.dot(normed_all, projection, preferred_element_type=jnp.float32)
    row_ids = jnp.arange(normed_all.shape[0], dtype=jnp.int32)
    seq_ids = row_ids // tok_rows
    row_positions = mp_index * tok_rows + row_ids % tok_rows
    limits = jnp.sum(
        jnp.where(
            seq_ids[:, None] == jnp.arange(lengths.shape[0], dtype=jnp.int32)[None, :],
            lengths[None, :],
            0,
        ),
        axis=1,
    )
    live_rows = (row_positions < limits)[:, None]
    difference = jnp.where(live_rows, predicted - targets.astype(jnp.float32), 0.0)
    live_count = jnp.sum(lengths).astype(jnp.float32)
    squared = lax.psum(jnp.sum(difference * difference), ("grp", "dp", "mp"))
    distill_loss = squared / (live_count * D_T)
    grad_pred = difference.astype(jnp.bfloat16)
    grad_proj = (
        lax.psum_scatter(
            lax.dot_general(
                normed_all, grad_pred, (((0,), (0,)), ((), ())), preferred_element_type=jnp.float32
            ).astype(jnp.bfloat16),
            "mp",
            scatter_dimension=0,
            tiled=True,
        ).astype(jnp.float32)
        / live_count
    )
    partial_grad = lax.psum_scatter(
        lax.dot_general(
            grad_pred, projection, (((1,), (1,)), ((), ())), preferred_element_type=jnp.float32
        ).astype(jnp.bfloat16),
        "dp",
        scatter_dimension=0,
        tiled=True,
    )
    width_half = norm_gain.shape[0] // 2
    gain_half = lax.dynamic_slice_in_dim(norm_gain, grp_index * width_half, width_half, 0)
    unit_half = lax.dynamic_slice_in_dim(unit_rows, grp_index * width_half, width_half, 1)
    grad_normed = lax.psum(partial_grad, "grp").astype(jnp.float32)
    inner_sum = jnp.sum(grad_normed * norm_gain * unit_rows, axis=-1, keepdims=True)
    grad_half = lax.dynamic_slice_in_dim(grad_normed, grp_index * width_half, width_half, 1)
    mean_term = inner_sum / D_S
    grad_hidden = inverse_rms * (grad_half * gain_half - unit_half * mean_term)
    grad_gain = lax.psum(jnp.sum(grad_half * unit_half, axis=0), ("dp", "mp")) / live_count
    return (own_target[None], distill_loss, grad_proj, grad_gain, grad_hidden[None])


def solution(mesh):
    in_specs = (
        P("dp", None, "mp"),
        P("dp", None, None),
        P("dp", None, None),
        P("mp", None),
        P("dp", "mp", None),
        P("dp", "mp", None),
        P(),
        P(None, ("grp", "dp")),
        P(),
    )
    out_specs = (P("dp", "mp", "grp"), P(), P("mp", ("grp", "dp")), P("grp"), P("dp", "mp", "grp"))
    return jax.shard_map(body, mesh=mesh, in_specs=in_specs, out_specs=out_specs, check_vma=False)
```

profile of v0, /device:TPU:0, one launch (start us, length us, event | category | flops | bytes accessed | tf_op | source)
XLA Modules:
  0.0 313.8 jit_solution(10362744790101362143)
XLA Ops:
  8.1 16.9 %conditional.2 = (bf16[512,1024]{0,1:T(8,128)(2,1)}) conditional(s32[]{:T(128)} %convert_element_type.80, () %tuple.33, (s32[512]{0:T(512)S(1)}, s32[]{:T(128)}, pred[]{:T(512)}, pred[]{:T(512)}, s32[]{:T(128)}, /*index=5*/bf16[1,512,512]{2,1,0:T(8,128)(2,1)}, bf16[1,512,1024]{2,1,0:T(8,128)(2,1)}, bf16[1,512,512]{2,1,0:T(8,128)(2,1)}) %tuple.46), branch_computations={%region_0.1_spmd, %region_1.4_spmd.clone.clone} | conditional | flops 1091305984 | bytes 39618764 | solution.py:66
  8.1 1.6 copy.35
  9.8 2.2 fusion.7
  12.1 5.7 %fusion.29 = (f32[8,512]{1,0:T(8,128)S(1)}, f32[8,512,512]{1,2,0:T(8,128)}) fusion(f32[512,512,8]{1,0,2:T(8,128)S(1)} %fusion.7, pred[512,512]{0,1:T(8,128)(4,1)S(1)} %iota_compare_fusion), kind=kOutput, calls=%fused_computation.57 | output fusion | flops 12583423 | bytes 17055744 | tf_op jit(solution)/shard_map/cond/branch_1_fun/while/body/eval_jaxpr/sub | solution.py:36
  17.8 2.0 copy.34
  19.9 5.2 %fusion.6 = bf16[8,512,128]{1,2,0:T(8,128)(2,1)} fusion(f32[8,512,512]{1,2,0:T(8,128)} %get-tuple-element.234, f32[8,512]{1,0:T(8,128)S(1)} %get-tuple-element.233, bf16[1,512,512]{1,2,0:T(8,128)(2,1)} %copy.34, s32[]{:T(128)S(6)} %select_n.74), kind=kOutput, calls=%fused_computation.9 | convolution fusion | flops 541589504 | bytes 9584644 | tf_op jit(solution)/shard_map/cond/branch_1_fun/while/body/eval_jaxpr/hbk,kd->bhd/dot_general | solution.py:38
  25.0 10.2 %conditional.3 = (bf16[512,5120]{1,0:T(8,128)(2,1)}) conditional(s32[]{:T(128)} %convert_element_type.80, () %tuple.32, (bf16[512,1024]{0,1:T(8,128)(2,1)}, bf16[1024,5120]{1,0:T(8,128)(2,1)}) %tuple.35), branch_computations={%region_4.5_spmd, %region_5.6_spmd} | conditional | flops 5368709120 | bytes 16777224 | solution.py:72
  25.0 10.1 %fusion.30 = bf16[512,5120]{1,0:T(8,128)(2,1)} fusion(bf16[512,1024]{0,1:T(8,128)(2,1)} %get-tuple-element.210, bf16[1024,5120]{1,0:T(8,128)(2,1)} %get-tuple-element.175), kind=kOutput, calls=%fused_computation.58 | convolution fusion | flops 5368709120 | bytes 16777216 | tf_op jit(solution)/shard_map/cond/branch_1_fun/dot_general | solution.py:74
  36.6 2.2 multiply_convert_fusion
  38.8 92.1 %reduce-scatter.4.cloned.1.call-done = bf16[128,5120]{1,0:T(8,128)(2,1)} async-done(((bf16[512,5120]{1,0:T(8,128)(2,1)}), bf16[128,5120]{1,0:T(8,128)(2,1)}) %reduce-scatter.4.cloned.1.call-update) | async-done | bytes 1310736 | tf_op jit(solution)/shard_map/reduce_scatter | solution.py:71
  130.9 2.0 fusion.17
  133.0 3.4 %collective-permute-start = (bf16[128,2560]{1,0:T(8,128)(2,1)S(1)}, bf16[128,2560]{1,0:T(8,128)(2,1)S(1)}, u32[]{:S(2)}, u32[]{:S(2)}) collective-permute-start(bf16[128,2560]{1,0:T(8,128)(2,1)S(1)} %slice.9), channel_id=1, source_target_pairs={{0,16},{1,17},{2,18},{3,19},{4,20},{5,21},{6,22},{7,23},{8,24},{9,... | collective-permute-start | bytes 1966088 | tf_op jit(solution)/shard_map/ppermute | solution.py:16
  136.4 14.0 %collective-permute-done = bf16[128,2560]{1,0:T(8,128)(2,1)S(1)} collective-permute-done((bf16[128,2560]{1,0:T(8,128)(2,1)S(1)}, bf16[128,2560]{1,0:T(8,128)(2,1)S(1)}, u32[]{:S(2)}, u32[]{:S(2)}) %collective-permute-start) | collective-permute-done | bytes 655392 | tf_op jit(solution)/shard_map/ppermute | solution.py:16
  152.2 4.2 %all-to-all-start = ((bf16[128,4,640]{2,0,1:T(8,128)(2,1)}), bf16[128,4,640]{2,0,1:T(8,128)(2,1)}, u32[]{:S(2)}, u32[]{:S(2)}) async-start(bf16[128,4,640]{2,0,1:T(8,128)(2,1)} %bitcast.61), calls=%async_computation.1 | async-start | bytes 1310720 | tf_op jit(solution)/shard_map/all_to_all | solution.py:89
  156.7 10.0 %all-to-all-done = bf16[128,4,640]{2,0,1:T(8,128)(2,1)} async-done(((bf16[128,4,640]{2,0,1:T(8,128)(2,1)}), bf16[128,4,640]{2,0,1:T(8,128)(2,1)}, u32[]{:S(2)}, u32[]{:S(2)}) %all-to-all-start) | async-done | bytes 655392 | tf_op jit(solution)/shard_map/all_to_all | solution.py:89
  166.7 2.2 convert_element_type.103
  168.9 5.0 %multiply_reduce_fusion.1 = (f32[]{:T(128)}, bf16[512,640]{1,0:T(8,128)(2,1)S(1)}) fusion(f32[512,640]{1,0:T(8,128)} %bitcast.62, bf16[512,2560]{1,0:T(8,128)(2,1)} %all-gather.2.cloned.1.call-done, bf16[2560,640]{1,0:T(8,128)(2,1)S(1)} %copy-done, pred[512]{0:T(512)(128)(4,1)S(1)} %fusion.23), kind=kOutput, calls=%fused_computation.32 | convolution fusion | flops 1679360000 | bytes 7864836 | tf_op jit(solution)/shard_map/dot_general | solution.py:90
  174.7 3.7 %convolution_convert_fusion.1 = bf16[512,2560]{1,0:T(8,128)(2,1)} fusion(bf16[2560,640]{1,0:T(8,128)(2,1)S(1)} %copy-done, bf16[512,640]{1,0:T(8,128)(2,1)S(1)} %get-tuple-element.240), kind=kOutput, calls=%fused_computation.22 | convolution fusion | flops 1679032320 | bytes 6553600 | tf_op jit(solution)/shard_map/dot_general | solution.py:120
  178.5 35.3 %reduce-scatter.8.cloned.1.call-done = bf16[128,2560]{1,0:T(8,128)(2,1)} async-done(((bf16[512,2560]{1,0:T(8,128)(2,1)}), bf16[128,2560]{1,0:T(8,128)(2,1)}) %reduce-scatter.8.cloned.1.call-update) | async-done | bytes 655376 | tf_op jit(solution)/shard_map/reduce_scatter | solution.py:119
  213.9 5.8 %convolution_convert_fusion = bf16[2560,640]{1,0:T(8,128)(2,1)} fusion(bf16[512,2560]{1,0:T(8,128)(2,1)} %all-gather.2.cloned.1.call-done, bf16[512,640]{1,0:T(8,128)(2,1)} %copy-done.4), kind=kOutput, calls=%fused_computation.21 | convolution fusion | flops 1679360000 | bytes 6553600 | tf_op jit(solution)/shard_map/dot_general | solution.py:110
  221.1 44.3 %psum.21 = f32[]{:T(128)} all-reduce(f32[]{:T(128)} %get-tuple-element.239), channel_id=1, replica_groups=mesh['grp'=2,'dp'=4,'mp'=4] {'grp','dp','mp'}, use_global_device_ids=true, to_apply=%region_10.11 | all-reduce | flops 1 | bytes 8 | tf_op jit(solution)/shard_map/psum | solution.py:105
  267.3 1.7 multiply_reduce_fusion
  270.0 32.0 %psum.23 = f32[1280]{0:T(1024)S(1)} all-reduce(f32[1280]{0:T(1024)S(1)} %get-tuple-element.236), channel_id=1, replica_groups=mesh['grp'=2,'dp'=4,'mp'=4] {'dp','mp'}, use_global_device_ids=true, to_apply=%region_16.17 | all-reduce | flops 1280 | bytes 10240 | tf_op jit(solution)/shard_map/psum | solution.py:135
  302.6 2.4 convert_divide_fusion
  (39 shorter events, 8.4 us)
Async XLA Ops:
  8.0 160.9 %copy-start = (bf16[2560,640]{1,0:T(8,128)(2,1)S(1)}, bf16[2560,640]{1,0:T(8,128)(2,1)}, u32[]{:S(2)}) copy-start(bf16[2560,640]{1,0:T(8,128)(2,1)} %param.20) | copy-start | bytes 9830404
  8.0 122.9 %reduce-scatter.4.cloned.1.call-start = ((), (), s32[]{:S(2)}) async-start(), calls=%async_computation.4 | async-start | bytes 6553600 | tf_op jit(solution)/shard_map/reduce_scatter | solution.py:71
  35.2 1.4 copy-start.2
  35.2 133.7 %all-gather.2.cloned.1.call-start = ((), (), s32[]{:S(2)}) async-start(), calls=%async_computation.5 | async-start | bytes 3276800 | tf_op jit(solution)/shard_map/all_gather | solution.py:88
  132.9 23.7 %copy-start.3 = (s32[4]{0:T(128)S(1)}, s32[4]{0:T(128)}, u32[]{:S(2)}) copy-start(s32[4]{0:T(128)} %param.21) | copy-start | bytes 52
  133.0 17.4 %collective-permute-start = (bf16[128,2560]{1,0:T(8,128)(2,1)S(1)}, bf16[128,2560]{1,0:T(8,128)(2,1)S(1)}, u32[]{:S(2)}, u32[]{:S(2)}) collective-permute-start(bf16[128,2560]{1,0:T(8,128)(2,1)S(1)} %slice.9), channel_id=1, source_target_pairs={{0,16},{1,17},{2,18},{3,19},{4,20},{5,21},{6,22},{7,23},{8,24},{9,... | collective-permute-start | bytes 1966088 | tf_op jit(solution)/shard_map/ppermute | solution.py:16
  150.5 0.8 copy-start.1
  152.2 14.5 %all-to-all-start = ((bf16[128,4,640]{2,0,1:T(8,128)(2,1)}), bf16[128,4,640]{2,0,1:T(8,128)(2,1)}, u32[]{:S(2)}, u32[]{:S(2)}) async-start(bf16[128,4,640]{2,0,1:T(8,128)(2,1)} %bitcast.61), calls=%async_computation.1 | async-start | bytes 1310720 | tf_op jit(solution)/shard_map/all_to_all | solution.py:89
  156.4 57.5 %reduce-scatter.8.cloned.1.call-start = ((), (), s32[]{:S(2)}) async-start(), calls=%async_computation.7 | async-start | bytes 3276800 | tf_op jit(solution)/shard_map/reduce_scatter | solution.py:119
  173.9 0.8 copy-start.4
  178.5 87.6 %all-reduce.2.cloned.1.call-start = ((), (), s32[]{:S(2)}) async-start(), calls=%async_computation.8 | async-start | bytes 1310720 | tf_op jit(solution)/shard_map/psum | solution.py:130
  213.9 88.8 %reduce-scatter.6.cloned.1.call-start = ((), (), s32[]{:S(2)}) async-start(), calls=%async_computation.6 | async-start | bytes 4096000 | tf_op jit(solution)/shard_map/reduce_scatter | solution.py:109
Sparse Core Ops, SparseCore 0:
  35.3 95.5 reduce-scatter.3
  219.9 63.9 reduce-scatter.5
Sparse Core Ops, SparseCore 1:
  38.8 27.1 all-gather.1
  178.6 35.2 reduce-scatter.7
  216.1 31.8 all-reduce.1
where the time goes:
time: 314 us
  waiting for transfers between devices  151 us (48%)
  blocking collectives  76.3 us (24%)
  matrix products  32 us (10%)
  other arithmetic  21.4 us (7%)
  between operations  18.2 us (6%)
  starting transfers between devices  7.96 us (3%)
  local copies, waits for them, and re-layouts  6.39 us (2%)
    reduce_scatter x1, waiting for transfers between devices, body(): lax.psum_scatter(lax.cond(grp_index == 0, lambda: jnp.dot(context, out_we...  92.1 us
    psum x1, blocking collectives, body(): squared = lax.psum(jnp.sum(difference * difference), ('grp', 'dp', 'mp'))  44.3 us
    reduce_scatter x1, waiting for transfers between devices, body(): lax.psum_scatter(lax.dot_general(grad_pred, projection, (((1,), (1,)), ((...  35.3 us
    psum x1, blocking collectives, body(): lax.psum(jnp.sum(grad_half * unit_half, axis=0), ('dp', 'mp')) / live_count  32 us
    ppermute x1, waiting for transfers between devices, passed_along(): return lax.ppermute(array, axis, pairs)  14 us
    dot_general x1, matrix products, body(): jnp.dot(context, out_weight, preferred_element_type=jnp.float32)  10.1 us
    all_to_all x1, waiting for transfers between devices, body(): lax.all_to_all(own_target, 'dp', split_axis=1, concat_axis=0, tiled=True)  9.96 us
  transfers between devices with their start and end apart: 7, of which 4 were waited for; matrix products, arithmetic and copies ran while one was open for 6% of the time, Pallas kernels for 0%

commit v1 on v0

v1 whole, which is shorter than its diff:
```python
import jax
import jax.numpy as jnp
from jax import lax
from jax.experimental import pallas as pl
from jax.experimental.pallas import tpu as pltpu
from jax.sharding import PartitionSpec as P

D_T = 5120
D_S = 2560
HD = 128
HQ = 32
KVH = 4
BF = jnp.bfloat16
F32 = jnp.float32


def swap(array, axis, flip):
    return lax.ppermute(array, axis, [(i, i ^ flip) for i in range(lax.axis_size(axis))])


def attend_kernel(q_ref, k_ref, v_ref, o_ref):
    rows, keys = q_ref.shape[0], k_ref.shape[0]
    scores = lax.dot_general(
        q_ref[...], k_ref[...], (((1,), (1,)), ((), ())), preferred_element_type=F32
    ) * (HD ** (-0.5))
    row_ids = pl.program_id(1) * rows + lax.broadcasted_iota(jnp.int32, (rows, keys), 0)
    key_ids = lax.broadcasted_iota(jnp.int32, (rows, keys), 1)
    scores = jnp.where(row_ids >= key_ids, scores, -1e30)
    exponent = jnp.exp(scores - jnp.max(scores, axis=-1, keepdims=True))
    total = jnp.sum(exponent, axis=-1, keepdims=True)
    weights = (exponent * (1.0 / total)).astype(BF)
    o_ref[...] = jnp.dot(weights, v_ref[...], preferred_element_type=F32).astype(BF)


def attend(queries, key_rows, value_rows):
    rows, width = queries.shape
    block = min(256, rows)
    keys = key_rows.shape[0]
    whole = pl.BlockSpec((keys, HD), lambda h, b: (0, 0))
    tile = pl.BlockSpec((block, HD), lambda h, b: (b, h))
    return pl.pallas_call(
        attend_kernel,
        grid=(width // HD, rows // block),
        in_specs=[tile, whole, whole],
        out_specs=tile,
        out_shape=jax.ShapeDtypeStruct((rows, width), BF),
        compiler_params=pltpu.CompilerParams(vmem_limit_bytes=32 * 1024 * 1024),
        cost_estimate=pl.CostEstimate(
            flops=4 * rows * keys * width,
            bytes_accessed=4 * rows * width + 4 * keys * HD,
            transcendentals=rows * keys * (width // HD),
        ),
    )(queries, key_rows, value_rows)


def line_scatter_sum(parts, axis, subs):
    n = lax.axis_size(axis)
    me = lax.axis_index(axis)
    rows = parts.shape[0] // n
    cols = parts.shape[1] // subs

    def term(block, sub):
        start = lax.rem(block + n, n) * rows
        return lax.dynamic_slice(parts, (start, sub * cols), (rows, cols))

    ups, downs = [None] * subs, [None] * subs
    for t in range(1, n):
        up_pairs = [(i, i + 1) for i in range(t)]
        down_pairs = [(n - 1 - i, n - 2 - i) for i in range(t)]
        for sub in range(subs):
            up, down = term(me + n - t, sub), term(me + t - n, sub)
            if t > 1:
                up = (up.astype(F32) + ups[sub].astype(F32)).astype(BF)
                down = (down.astype(F32) + downs[sub].astype(F32)).astype(BF)
            ups[sub] = lax.ppermute(up, axis, up_pairs)
            downs[sub] = lax.ppermute(down, axis, down_pairs)
    sums = [
        term(me, sub).astype(F32) + ups[sub].astype(F32) + downs[sub].astype(F32)
        for sub in range(subs)
    ]
    return jnp.concatenate(sums, axis=1)


def body(
    queries, keys, values, out_weight, residual, student_hidden, norm_gain, projection, lengths
):
    tok_rows = residual.shape[1]
    half_cols = residual.shape[2] // 2
    width_half = norm_gain.shape[0] // 2
    shard_cols = projection.shape[1]
    grp = lax.axis_index("grp")
    dp = lax.axis_index("dp")
    mp = lax.axis_index("mp")
    dp_hi, dp_lo = dp // 2, dp % 2

    hidden = student_hidden[0].astype(F32)
    inverse_rms = lax.rsqrt(jnp.mean(hidden * hidden, axis=-1, keepdims=True) + 1e-06)
    normed = (hidden * inverse_rms * norm_gain).astype(BF)
    normed_pair = jnp.concatenate([normed, swap(normed, "dp", 2)], axis=0)
    normed_all = jnp.concatenate([normed_pair, swap(normed_pair, "dp", 1)], axis=0)

    local_heads = queries.shape[2] // HD
    kv_head = mp * local_heads // (HQ // KVH)
    key_rows = lax.dynamic_slice_in_dim(keys[0], kv_head * HD, HD, 1)
    value_rows = lax.dynamic_slice_in_dim(values[0], kv_head * HD, HD, 1)
    context = attend(queries[0], key_rows, value_rows)
    weight_half = lax.dynamic_slice_in_dim(out_weight, grp * half_cols, half_cols, 1)
    attn_part = jnp.dot(context, weight_half, preferred_element_type=F32).astype(BF)
    attn_rows = line_scatter_sum(attn_part, "mp", 2)
    residual_half = lax.dynamic_slice_in_dim(residual[0], grp * half_cols, half_cols, 1)
    own_target = (residual_half.astype(F32) + attn_rows).astype(BF)

    pair_cols = 2 * shard_cols
    kept = lax.dynamic_slice_in_dim(own_target, dp_hi * pair_cols, pair_cols, 1)
    sent = lax.dynamic_slice_in_dim(own_target, (1 - dp_hi) * pair_cols, pair_cols, 1)
    target_pair = jnp.concatenate([kept, swap(sent, "dp", 2)], axis=0)
    kept = lax.dynamic_slice_in_dim(target_pair, dp_lo * shard_cols, shard_cols, 1)
    sent = lax.dynamic_slice_in_dim(target_pair, (1 - dp_lo) * shard_cols, shard_cols, 1)
    targets = jnp.concatenate([kept, swap(sent, "dp", 1)], axis=0)

    predicted = jnp.dot(normed_all, projection, preferred_element_type=F32)
    position = mp * tok_rows + jnp.arange(tok_rows, dtype=jnp.int32)
    live_rows = jnp.concatenate([position < lengths[dp ^ flip] for flip in (0, 2, 1, 3)])
    difference = jnp.where(live_rows[:, None], predicted - targets.astype(F32), 0.0)
    live_count = jnp.sum(lengths).astype(F32)
    squared = jnp.sum(difference * difference)
    grad_pred = difference.astype(BF)

    def pull_back(rows):
        return lax.dot_general(
            rows, projection, (((1,), (1,)), ((), ())), preferred_element_type=F32
        )

    arrived = swap(pull_back(grad_pred[2 * tok_rows :]).astype(BF), "dp", 1)
    pulled = pull_back(grad_pred[: 2 * tok_rows]) + arrived.astype(F32)
    pulled = pulled.reshape(2, tok_rows, 2 * width_half)
    half_rows = tok_rows // 2

    def own_half(array):
        return lax.dynamic_slice_in_dim(array, grp * width_half, width_half, array.ndim - 1)

    def other_half(array):
        return lax.dynamic_slice_in_dim(array, (1 - grp) * width_half, width_half, array.ndim - 1)

    first = pulled[:, :half_rows]
    second = pulled[:, half_rows:]
    first_in = swap(first[1].astype(BF), "dp", 2)
    second_in = swap(other_half(second).astype(BF), "grp", 1)
    first = first[0] + first_in.astype(F32)
    second = own_half(second) + second_in.astype(F32)
    first_in = swap(other_half(first).astype(BF), "grp", 1)
    second_in = swap(second[1].astype(BF), "dp", 2)
    grad_half = jnp.concatenate(
        [own_half(first) + first_in.astype(F32), second[0] + second_in.astype(F32)], axis=0
    )

    grad_proj_part = lax.dot_general(
        normed_all, grad_pred, (((0,), (0,)), ((), ())), preferred_element_type=F32
    ).astype(BF)
    grad_proj = line_scatter_sum(grad_proj_part, "mp", 1) / live_count

    gain_half = own_half(norm_gain)
    unit_half = own_half(hidden) * inverse_rms
    scaled = grad_half * gain_half
    inner_sum = jnp.sum(scaled * unit_half, axis=-1)
    inner_sum = inner_sum + swap(inner_sum, "grp", 1)
    mean_term = inner_sum[:, None] / D_S
    grad_hidden = inverse_rms * (scaled - unit_half * mean_term)

    sums = jnp.concatenate(
        [jnp.sum(grad_half * unit_half, axis=0), jnp.full((128,), squared, F32)]
    )
    gathered = lax.all_gather(sums, ("grp", "dp", "mp"), axis=0, tiled=False)
    gathered = gathered.reshape(lax.axis_size("grp"), -1, width_half + 128)
    grad_gain = (
        jnp.sum(lax.dynamic_index_in_dim(gathered, grp, 0, False)[:, :width_half], axis=0)
        / live_count
    )
    distill_loss = jnp.sum(gathered[:, :, width_half]) / (live_count * D_T)
    return (own_target[None], distill_loss, grad_proj, grad_gain, grad_hidden[None])


def solution(mesh):
    in_specs = (
        P("dp", None, "mp"),
        P("dp", None, None),
        P("dp", None, None),
        P("mp", None),
        P("dp", "mp", None),
        P("dp", "mp", None),
        P(),
        P(None, ("grp", "dp")),
        P(),
    )
    out_specs = (P("dp", "mp", "grp"), P(), P("mp", ("grp", "dp")), P("grp"), P("dp", "mp", "grp"))
    return jax.shard_map(body, mesh=mesh, in_specs=in_specs, out_specs=out_specs, check_vma=False)
```

time: 314 us -> 282 us (0.90)
  waiting for transfers between devices: 151 us -> 64.8 us
  starting transfers between devices: 7.96 us -> 70.1 us
  between operations: 18.2 us -> 3.63 us
  other arithmetic: 21.4 us -> 35.6 us
  matrix products: 32 us -> 19 us
  Pallas kernels: 0 us -> 9.7 us
  blocking collectives: 76.3 us -> 68.4 us
  local copies, waits for them, and re-layouts: 6.39 us -> 10.2 us
    reduce_scatter x3 -> x0, waiting for transfers between devices: 127 us -> none  [the longest x1 92.1 us: body(): lax.psum_scatter(lax.cond(grp_index == 0, lambda: jnp.dot(context, out_we...]
    psum x2 -> x0, blocking collectives: 76.3 us -> none  [the longest x1 44.3 us: body(): squared = lax.psum(jnp.sum(difference * difference), ('grp', 'dp', 'mp'))]
    all_gather x0 -> x1, blocking collectives: none -> 68.4 us  [body(): gathered = lax.all_gather(sums, ('grp', 'dp', 'mp'), axis=0, tiled=False)]
    ppermute x1 -> x28, starting transfers between devices: 3.41 us -> 70.1 us  [the longest x9 47.7 us: line_scatter_sum(): ups[sub] = lax.ppermute(up, axis, up_pairs)]
    ppermute x1 -> x28, waiting for transfers between devices: 14 us -> 64.8 us  [the longest x9 40 us: line_scatter_sum(): ups[sub] = lax.ppermute(up, axis, up_pairs)]
    dot_general x5 -> x4, matrix products: 26.2 us -> 15.1 us  [the longest x1 5.58 us: body(): jnp.dot(context, weight_half, preferred_element_type=F32).astype(BF)]
    all_to_all x1 -> x0, waiting for transfers between devices: 9.96 us -> none  [body(): lax.all_to_all(own_target, 'dp', split_axis=1, concat_axis=0, tiled=True)]
    pallas_call x0 -> x1, Pallas kernels: none -> 9.7 us  [attend(): pl.pallas_call(attend_kernel, grid=(width // HD, rows // block), in_specs...]
  transfers between devices with their start and end apart: 7 -> 28, of which waited for: 4 -> 14; matrix products, arithmetic and copies ran while one was open for 6% -> 14% of each run, Pallas kernels for 0% -> 0%
where the time goes in v1:
time: 282 us; the launch traced here: 281 us
  starting transfers between devices  70.1 us (25%)
  blocking collectives  68.4 us (24%)
  waiting for transfers between devices  64.8 us (23%)
  other arithmetic  35.6 us (13%)
  matrix products  19 us (7%)
  local copies, waits for them, and re-layouts  10.2 us (4%)
  Pallas kernels  9.7 us (3%)
  between operations  3.63 us (1%)
    all_gather x1, blocking collectives, body(): gathered = lax.all_gather(sums, ('grp', 'dp', 'mp'), axis=0, tiled=False)  68.4 us
    ppermute x9, starting transfers between devices, line_scatter_sum(): ups[sub] = lax.ppermute(up, axis, up_pairs)  47.7 us
    ppermute x9, waiting for transfers between devices, line_scatter_sum(): ups[sub] = lax.ppermute(up, axis, up_pairs)  40 us
    ppermute x9, waiting for transfers between devices, line_scatter_sum(): downs[sub] = lax.ppermute(down, axis, down_pairs)  14.9 us
    ppermute x10, starting transfers between devices, swap(): lax.ppermute(array, axis, [(i, i ^ flip) for i in range(lax.axis_size(axi...  11.5 us
    ppermute x9, starting transfers between devices, line_scatter_sum(): downs[sub] = lax.ppermute(down, axis, down_pairs)  10.9 us
    ppermute x10, waiting for transfers between devices, swap(): lax.ppermute(array, axis, [(i, i ^ flip) for i in range(lax.axis_size(axi...  9.92 us
    pallas_call x1, Pallas kernels, attend(): pl.pallas_call(attend_kernel, grid=(width // HD, rows // block), in_specs...  9.7 us
  transfers between devices with their start and end apart: 28, of which 14 were waited for; matrix products, arithmetic and copies ran while one was open for 14% of the time, Pallas kernels for 0%

profile of v1, /device:TPU:0, one launch (start us, length us, event | category | flops | bytes accessed | tf_op | source)
XLA Modules:
  0.0 281.4 jit_solution(18017892262825815233)
XLA Ops:
  3.1 9.7 %shard_map.128 = bf16[512,1024]{1,0:T(8,128)(2,1)S(1)} custom-call(bf16[512,1024]{1,0:T(8,128)(2,1)S(1)} %bitcast.57, bf16[512,128]{1,0:T(8,128)(2,1)S(1)} %get-tuple-element.34.k_ref, bf16[512,128]{1,0:T(8,128)(2,1)S(1)} %get-tuple-element.33.v_ref), custom_call_target="tpu_custom_call" | custom-call | flops 1073741824 | bytes 2359296 | tf_op jit(solution)/shard_map/pallas_call | solution.py:41
  12.8 5.6 %fusion.2 = bf16[512,2560]{1,0:T(8,128)(2,1)S(1)} fusion(bf16[512,1024]{1,0:T(8,128)(2,1)S(1)} %shard_map.128, bf16[1024,5120]{1,0:T(8,128)(2,1)} %param.12, s32[]{:T(128)S(6)} %select_n.113), kind=kOutput, calls=%fused_computation.3 | convolution fusion | flops 2685665280 | bytes 8912900 | tf_op jit(solution)/shard_map/dot_general | solution.py:108
  20.9 5.7 %collective-permute-start = (bf16[128,1280]{1,0:T(8,128)(2,1)}, bf16[128,1280]{1,0:T(8,128)(2,1)}, u32[]{:S(2)}, u32[]{:S(2)}) collective-permute-start(bf16[128,1280]{1,0:T(8,128)(2,1)} %get-tuple-element.16), channel_id=1, source_target_pairs={{0,1},{4,5},{8,9},{12,13},{16,17},{20,21},{24,25},{28,29}} | collective-permute-start | bytes 983048 | tf_op jit(solution)/shard_map/ppermute | solution.py:75
  28.0 5.2 %collective-permute-done = bf16[128,1280]{1,0:T(8,128)(2,1)} collective-permute-done((bf16[128,1280]{1,0:T(8,128)(2,1)}, bf16[128,1280]{1,0:T(8,128)(2,1)}, u32[]{:S(2)}, u32[]{:S(2)}) %collective-permute-start) | collective-permute-done | bytes 327712 | tf_op jit(solution)/shard_map/ppermute | solution.py:75
  35.0 5.1 %collective-permute-start.1 = (bf16[128,1280]{1,0:T(8,128)(2,1)}, bf16[128,1280]{1,0:T(8,128)(2,1)}, u32[]{:S(2)}, u32[]{:S(2)}) collective-permute-start(bf16[128,1280]{1,0:T(8,128)(2,1)} %add_convert_fusion.11), channel_id=1, source_target_pairs={{0,1},{1,2},{4,5},{5,6},{8,9},{9,10},{12,13},{13,14},{16,17},{17,1... | collective-permute-start | bytes 983048 | tf_op jit(solution)/shard_map/ppermute | solution.py:75
  40.1 5.7 %collective-permute-done.1 = bf16[128,1280]{1,0:T(8,128)(2,1)} collective-permute-done((bf16[128,1280]{1,0:T(8,128)(2,1)}, bf16[128,1280]{1,0:T(8,128)(2,1)}, u32[]{:S(2)}, u32[]{:S(2)}) %collective-permute-start.1) | collective-permute-done | bytes 327712 | tf_op jit(solution)/shard_map/ppermute | solution.py:75
  49.4 5.0 %collective-permute-start.6 = (bf16[128,1280]{1,0:T(8,128)(2,1)}, bf16[128,1280]{1,0:T(8,128)(2,1)}, u32[]{:S(2)}, u32[]{:S(2)}) collective-permute-start(bf16[128,1280]{1,0:T(8,128)(2,1)} %get-tuple-element.18), channel_id=1, source_target_pairs={{0,1},{4,5},{8,9},{12,13},{16,17},{20,21},{24,25},{28,29}} | collective-permute-start | bytes 983048 | tf_op jit(solution)/shard_map/ppermute | solution.py:75
  62.2 4.0 %collective-permute-done.2 = bf16[128,1280]{1,0:T(8,128)(2,1)S(1)} collective-permute-done((bf16[128,1280]{1,0:T(8,128)(2,1)}, bf16[128,1280]{1,0:T(8,128)(2,1)S(1)}, u32[]{:S(2)}, u32[]{:S(2)}) %collective-permute-start.2) | collective-permute-done | bytes 327712 | tf_op jit(solution)/shard_map/ppermute | solution.py:75
  68.5 2.6 convert_add_fusion.4
  72.5 5.6 %collective-permute-start.7 = (bf16[128,1280]{1,0:T(8,128)(2,1)}, bf16[128,1280]{1,0:T(8,128)(2,1)}, u32[]{:S(2)}, u32[]{:S(2)}) collective-permute-start(bf16[128,1280]{1,0:T(8,128)(2,1)} %get-tuple-element.13), channel_id=1, source_target_pairs={{0,1},{1,2},{4,5},{5,6},{8,9},{9,10},{12,13},{13,14},{16,17},{17,1... | collective-permute-start | bytes 983048 | tf_op jit(solution)/shard_map/ppermute | solution.py:75
  85.0 6.8 %collective-permute-start.8 = (bf16[128,1280]{1,0:T(8,128)(2,1)S(1)}, bf16[128,1280]{1,0:T(8,128)(2,1)S(1)}, u32[]{:S(2)}, u32[]{:S(2)}) collective-permute-start(bf16[128,1280]{1,0:T(8,128)(2,1)S(1)} %get-tuple-element.20), channel_id=1, source_target_pairs={{0,1},{1,2},{2,3},{4,5},{5,6},{6,7},{8,9},{9,10},{10,11},{12,13},{... | collective-permute-start | bytes 983048 | tf_op jit(solution)/shard_map/ppermute | solution.py:75
  100.7 6.2 %collective-permute-done.14 = bf16[128,1280]{1,0:T(8,128)(2,1)} collective-permute-done((bf16[128,1280]{1,0:T(8,128)(2,1)}, bf16[128,1280]{1,0:T(8,128)(2,1)}, u32[]{:S(2)}, u32[]{:S(2)}) %collective-permute-start.14) | collective-permute-done | bytes 327712 | tf_op jit(solution)/shard_map/ppermute | solution.py:18
  110.7 4.6 %multiply_reduce_fusion = (f32[]{:T(128)}, bf16[512,640]{1,0:T(8,128)(2,1)S(1)}) fusion(bf16[256,640]{1,0:T(8,128)(2,1)S(1)} %collective-permute-done.15, bf16[256,640]{1,0:T(8,128)(2,1)S(1)} %get-tuple-element.24, bf16[2560,640]{1,0:T(8,128)(2,1)S(1)} %copy-done, bf16[256,2560]{1,0:T(8,128)(2,1)} %collective-permute-done.13, ...), kind=kOutput, calls=%fused_computation.25 | convolution fusion | flops 1688535040 | bytes 7209476 | tf_op jit(solution)/shard_map/dot_general | solution.py:121
  118.1 3.9 %convolution_convert_fusion = bf16[2560,640]{1,0:T(8,128)(2,1)S(1)} fusion(bf16[512,640]{1,0:T(8,128)(2,1)S(1)} %get-tuple-element.23, bf16[256,2560]{1,0:T(8,128)(2,1)} %collective-permute-done.13, bf16[128,2560]{1,0:T(8,128)(2,1)} %collective-permute-done.12, bf16[128,2560]{1,0:T(8,128)(2,1)} %fusion.11), kind=kOutput, calls=%fused_computation.2 | convolution fusion | flops 1687224320 | bytes 6553600 | tf_op jit(solution)/shard_map/dot_general | solution.py:157
  124.3 7.7 %collective-permute-start.21 = (bf16[640,640]{1,0:T(8,128)(2,1)}, bf16[640,640]{1,0:T(8,128)(2,1)}, u32[]{:S(2)}, u32[]{:S(2)}) collective-permute-start(bf16[640,640]{1,0:T(8,128)(2,1)} %get-tuple-element.9), channel_id=1, source_target_pairs={{0,1},{4,5},{8,9},{12,13},{16,17},{20,21},{24,25},{28,29}} | collective-permute-start | bytes 2457608 | tf_op jit(solution)/shard_map/ppermute | solution.py:75
  135.7 2.5 fusion.6
  139.0 10.0 %collective-permute-done.21 = bf16[640,640]{1,0:T(8,128)(2,1)} collective-permute-done((bf16[640,640]{1,0:T(8,128)(2,1)}, bf16[640,640]{1,0:T(8,128)(2,1)}, u32[]{:S(2)}, u32[]{:S(2)}) %collective-permute-start.21) | collective-permute-done | bytes 819232 | tf_op jit(solution)/shard_map/ppermute | solution.py:75
  150.6 4.6 %collective-permute-start.22 = (bf16[640,640]{1,0:T(8,128)(2,1)S(1)}, bf16[640,640]{1,0:T(8,128)(2,1)S(1)}, u32[]{:S(2)}, u32[]{:S(2)}) collective-permute-start(bf16[640,640]{1,0:T(8,128)(2,1)S(1)} %add_convert_fusion.3), channel_id=1, source_target_pairs={{0,1},{1,2},{4,5},{5,6},{8,9},{9,10},{12,13},{13,14},{16,17},{17,1... | collective-permute-start | bytes 2457608 | tf_op jit(solution)/shard_map/ppermute | solution.py:75
  155.3 2.6 convert_add_fusion
  161.2 10.6 %collective-permute-done.22 = bf16[640,640]{1,0:T(8,128)(2,1)S(1)} collective-permute-done((bf16[640,640]{1,0:T(8,128)(2,1)S(1)}, bf16[640,640]{1,0:T(8,128)(2,1)S(1)}, u32[]{:S(2)}, u32[]{:S(2)}) %collective-permute-start.22) | collective-permute-done | bytes 819232 | tf_op jit(solution)/shard_map/ppermute | solution.py:75
  173.9 5.9 %collective-permute-start.23 = (bf16[640,640]{1,0:T(8,128)(2,1)}, bf16[640,640]{1,0:T(8,128)(2,1)}, u32[]{:S(2)}, u32[]{:S(2)}) collective-permute-start(bf16[640,640]{1,0:T(8,128)(2,1)} %get-tuple-element.7), channel_id=1, source_target_pairs={{0,1},{1,2},{2,3},{4,5},{5,6},{6,7},{8,9},{9,10},{10,11},{12,13},{... | collective-permute-start | bytes 2457608 | tf_op jit(solution)/shard_map/ppermute | solution.py:75
  189.9 68.4 %all-gather.1 = f32[32,1,1408]{2,1,0:T(1,128)S(1)} all-gather(f32[1,1,1408]{2,1,0:T(1,128)S(1)} %reshape.45), channel_id=2, replica_groups=mesh['grp'=2,'dp'=4,'mp'=4] {'grp','dp','mp'}, dimensions={0}, use_global_device_ids=true | all-gather | bytes 185856 | tf_op jit(solution)/shard_map/all_gather | solution.py:173
  265.0 12.1 %collective-permute-done.26 = bf16[640,640]{1,0:T(8,128)(2,1)} collective-permute-done((bf16[640,640]{1,0:T(8,128)(2,1)}, bf16[640,640]{1,0:T(8,128)(2,1)}, u32[]{:S(2)}, u32[]{:S(2)}) %collective-permute-start.26) | collective-permute-done | bytes 819232 | tf_op jit(solution)/shard_map/ppermute | solution.py:76
  277.1 3.1 %add_divide_fusion = f32[640,640]{1,0:T(8,128)} fusion(bf16[640,640]{1,0:T(8,128)(2,1)} %collective-permute-done.26, bf16[640,640]{1,0:T(8,128)(2,1)} %collective-permute-done.23, f32[]{:T(128)S(6)} %convert_element_type.257, bf16[2560,640]{1,0:T(8,128)(2,1)} %copy-done.2, s32[]{:T(128)S(6)} %select_n.136), kind=kLoop, calls=%fused_computation.7 | loop fusion | flops 2457600 | bytes 4096008 | tf_op jit(solution)/shard_map/div | solution.py:160
  (120 shorter events, 74.6 us)
Async XLA Ops:
  20.9 12.2 %collective-permute-start = (bf16[128,1280]{1,0:T(8,128)(2,1)}, bf16[128,1280]{1,0:T(8,128)(2,1)}, u32[]{:S(2)}, u32[]{:S(2)}) collective-permute-start(bf16[128,1280]{1,0:T(8,128)(2,1)} %get-tuple-element.16), channel_id=1, source_target_pairs={{0,1},{4,5},{8,9},{12,13},{16,17},{20,21},{24,25},{28,29}} | collective-permute-start | bytes 983048 | tf_op jit(solution)/shard_map/ppermute | solution.py:75
  26.6 13.5 %collective-permute-start.3 = (bf16[128,1280]{1,0:T(8,128)(2,1)}, bf16[128,1280]{1,0:T(8,128)(2,1)}, u32[]{:S(2)}, u32[]{:S(2)}) collective-permute-start(bf16[128,1280]{1,0:T(8,128)(2,1)} %get-tuple-element.19), channel_id=1, source_target_pairs={{3,2},{7,6},{11,10},{15,14},{19,18},{23,22},{27,26},{31,30}} | collective-permute-start | bytes 983048 | tf_op jit(solution)/shard_map/ppermute | solution.py:76
  35.0 10.8 %collective-permute-start.1 = (bf16[128,1280]{1,0:T(8,128)(2,1)}, bf16[128,1280]{1,0:T(8,128)(2,1)}, u32[]{:S(2)}, u32[]{:S(2)}) collective-permute-start(bf16[128,1280]{1,0:T(8,128)(2,1)} %add_convert_fusion.11), channel_id=1, source_target_pairs={{0,1},{1,2},{4,5},{5,6},{8,9},{9,10},{12,13},{13,14},{16,17},{17,1... | collective-permute-start | bytes 983048 | tf_op jit(solution)/shard_map/ppermute | solution.py:75
  48.0 9.1 %collective-permute-start.4 = (bf16[128,1280]{1,0:T(8,128)(2,1)}, bf16[128,1280]{1,0:T(8,128)(2,1)}, u32[]{:S(2)}, u32[]{:S(2)}) collective-permute-start(bf16[128,1280]{1,0:T(8,128)(2,1)} %get-tuple-element.15), channel_id=1, source_target_pairs={{3,2},{2,1},{7,6},{6,5},{11,10},{10,9},{15,14},{14,13},{19,18},{18... | collective-permute-start | bytes 983048 | tf_op jit(solution)/shard_map/ppermute | solution.py:76
  49.4 12.8 %collective-permute-start.6 = (bf16[128,1280]{1,0:T(8,128)(2,1)}, bf16[128,1280]{1,0:T(8,128)(2,1)}, u32[]{:S(2)}, u32[]{:S(2)}) collective-permute-start(bf16[128,1280]{1,0:T(8,128)(2,1)} %get-tuple-element.18), channel_id=1, source_target_pairs={{0,1},{4,5},{8,9},{12,13},{16,17},{20,21},{24,25},{28,29}} | collective-permute-start | bytes 983048 | tf_op jit(solution)/shard_map/ppermute | solution.py:75
  55.8 10.4 %collective-permute-start.2 = (bf16[128,1280]{1,0:T(8,128)(2,1)}, bf16[128,1280]{1,0:T(8,128)(2,1)S(1)}, u32[]{:S(2)}, u32[]{:S(2)}) collective-permute-start(bf16[128,1280]{1,0:T(8,128)(2,1)} %get-tuple-element.14), channel_id=1, source_target_pairs={{0,1},{1,2},{2,3},{4,5},{5,6},{6,7},{8,9},{9,10},{10,11},{12,13},{... | collective-permute-start | bytes 983048 | tf_op jit(solution)/shard_map/ppermute | solution.py:75
  58.3 10.2 %collective-permute-start.5 = (bf16[128,1280]{1,0:T(8,128)(2,1)S(1)}, bf16[128,1280]{1,0:T(8,128)(2,1)S(1)}, u32[]{:S(2)}, u32[]{:S(2)}) collective-permute-start(bf16[128,1280]{1,0:T(8,128)(2,1)S(1)} %add_convert_fusion.8), channel_id=1, source_target_pairs={{3,2},{2,1},{1,0},{7,6},{6,5},{5,4},{11,10},{10,9},{9,8},{15,14},{... | collective-permute-start | bytes 983048 | tf_op jit(solution)/shard_map/ppermute | solution.py:76
  71.1 9.6 %collective-permute-start.10 = (bf16[128,1280]{1,0:T(8,128)(2,1)}, bf16[128,1280]{1,0:T(8,128)(2,1)}, u32[]{:S(2)}, u32[]{:S(2)}) collective-permute-start(bf16[128,1280]{1,0:T(8,128)(2,1)} %get-tuple-element.12), channel_id=1, source_target_pairs={{3,2},{2,1},{7,6},{6,5},{11,10},{10,9},{15,14},{14,13},{19,18},{18... | collective-permute-start | bytes 983048 | tf_op jit(solution)/shard_map/ppermute | solution.py:76
  72.5 9.7 %collective-permute-start.7 = (bf16[128,1280]{1,0:T(8,128)(2,1)}, bf16[128,1280]{1,0:T(8,128)(2,1)}, u32[]{:S(2)}, u32[]{:S(2)}) collective-permute-start(bf16[128,1280]{1,0:T(8,128)(2,1)} %get-tuple-element.13), channel_id=1, source_target_pairs={{0,1},{1,2},{4,5},{5,6},{8,9},{9,10},{12,13},{13,14},{16,17},{17,1... | collective-permute-start | bytes 983048 | tf_op jit(solution)/shard_map/ppermute | solution.py:75
  79.1 12.7 %collective-permute-start.12 = (bf16[128,2560]{1,0:T(8,128)(2,1)}, bf16[128,2560]{1,0:T(8,128)(2,1)}, u32[]{:S(2)}, u32[]{:S(2)}) collective-permute-start(bf16[128,2560]{1,0:T(8,128)(2,1)} %fusion.11), channel_id=1, source_target_pairs={{0,8},{4,12},{8,0},{12,4},{1,9},{5,13},{9,1},{13,5},{2,10},{6,14},... | collective-permute-start | bytes 1966088 | tf_op jit(solution)/shard_map/ppermute | solution.py:18
  83.6 11.1 %collective-permute-start.11 = (bf16[128,1280]{1,0:T(8,128)(2,1)S(1)}, bf16[128,1280]{1,0:T(8,128)(2,1)S(1)}, u32[]{:S(2)}, u32[]{:S(2)}) collective-permute-start(bf16[128,1280]{1,0:T(8,128)(2,1)S(1)} %get-tuple-element.21), channel_id=1, source_target_pairs={{3,2},{2,1},{1,0},{7,6},{6,5},{5,4},{11,10},{10,9},{9,8},{15,14},{... | collective-permute-start | bytes 983048 | tf_op jit(solution)/shard_map/ppermute | solution.py:76
  85.0 11.4 %collective-permute-start.8 = (bf16[128,1280]{1,0:T(8,128)(2,1)S(1)}, bf16[128,1280]{1,0:T(8,128)(2,1)S(1)}, u32[]{:S(2)}, u32[]{:S(2)}) collective-permute-start(bf16[128,1280]{1,0:T(8,128)(2,1)S(1)} %get-tuple-element.20), channel_id=1, source_target_pairs={{0,1},{1,2},{2,3},{4,5},{5,6},{6,7},{8,9},{9,10},{10,11},{12,13},{... | collective-permute-start | bytes 983048 | tf_op jit(solution)/shard_map/ppermute | solution.py:75
  94.2 16.4 %collective-permute-start.13 = (bf16[256,2560]{1,0:T(8,128)(2,1)}, bf16[256,2560]{1,0:T(8,128)(2,1)}, u32[]{:S(2)}, u32[]{:S(2)}) collective-permute-start(bf16[256,2560]{1,0:T(8,128)(2,1)} %pad_maximum_fusion.1), channel_id=1, source_target_pairs={{0,4},{4,0},{8,12},{12,8},{1,5},{5,1},{9,13},{13,9},{2,6},{6,2},{1... | collective-permute-start | bytes 3932168 | tf_op jit(solution)/shard_map/ppermute | solution.py:18
  98.5 8.3 %collective-permute-start.14 = (bf16[128,1280]{1,0:T(8,128)(2,1)}, bf16[128,1280]{1,0:T(8,128)(2,1)}, u32[]{:S(2)}, u32[]{:S(2)}) collective-permute-start(bf16[128,1280]{1,0:T(8,128)(2,1)} %get-tuple-element.26), channel_id=1, source_target_pairs={{0,8},{4,12},{8,0},{12,4},{1,9},{5,13},{9,1},{13,5},{2,10},{6,14},... | collective-permute-start | bytes 983048 | tf_op jit(solution)/shard_map/ppermute | solution.py:18
  117.6 37.6 %collective-permute-start.16 = (bf16[256,2560]{1,0:T(8,128)(2,1)}, bf16[256,2560]{1,0:T(8,128)(2,1)}, u32[]{:S(2)}, u32[]{:S(2)}) collective-permute-start(bf16[256,2560]{1,0:T(8,128)(2,1)} %convolution_convert_fusion.1), channel_id=1, source_target_pairs={{0,4},{4,0},{8,12},{12,8},{1,5},{5,1},{9,13},{13,9},{2,6},{6,2},{1... | collective-permute-start | bytes 3932168 | tf_op jit(solution)/shard_map/ppermute | solution.py:18
  124.3 24.8 %collective-permute-start.21 = (bf16[640,640]{1,0:T(8,128)(2,1)}, bf16[640,640]{1,0:T(8,128)(2,1)}, u32[]{:S(2)}, u32[]{:S(2)}) collective-permute-start(bf16[640,640]{1,0:T(8,128)(2,1)} %get-tuple-element.9), channel_id=1, source_target_pairs={{0,1},{4,5},{8,9},{12,13},{16,17},{20,21},{24,25},{28,29}} | collective-permute-start | bytes 2457608 | tf_op jit(solution)/shard_map/ppermute | solution.py:75
  138.2 23.1 %collective-permute-start.24 = (bf16[640,640]{1,0:T(8,128)(2,1)S(1)}, bf16[640,640]{1,0:T(8,128)(2,1)S(1)}, u32[]{:S(2)}, u32[]{:S(2)}) collective-permute-start(bf16[640,640]{1,0:T(8,128)(2,1)S(1)} %copy-done.12), channel_id=1, source_target_pairs={{3,2},{7,6},{11,10},{15,14},{19,18},{23,22},{27,26},{31,30}} | collective-permute-start | bytes 2457608 | tf_op jit(solution)/shard_map/ppermute | solution.py:76
  150.6 21.2 %collective-permute-start.22 = (bf16[640,640]{1,0:T(8,128)(2,1)S(1)}, bf16[640,640]{1,0:T(8,128)(2,1)S(1)}, u32[]{:S(2)}, u32[]{:S(2)}) collective-permute-start(bf16[640,640]{1,0:T(8,128)(2,1)S(1)} %add_convert_fusion.3), channel_id=1, source_target_pairs={{0,1},{1,2},{4,5},{5,6},{8,9},{9,10},{12,13},{13,14},{16,17},{17,1... | collective-permute-start | bytes 2457608 | tf_op jit(solution)/shard_map/ppermute | solution.py:75
  158.0 21.8 %collective-permute-start.19 = (bf16[2,64,1280]{2,1,0:T(8,128)(2,1)S(1)}, bf16[2,64,1280]{2,1,0:T(8,128)(2,1)S(1)}, u32[]{:S(2)}, u32[]{:S(2)}) collective-permute-start(bf16[2,64,1280]{2,1,0:T(8,128)(2,1)S(1)} %dynamic-slice_convert_fusion), channel_id=1, source_target_pairs={{0,16},{16,0},{1,17},{17,1},{2,18},{18,2},{3,19},{19,3},{4,20},{20... | collective-permute-start | bytes 983048 | tf_op jit(solution)/shard_map/ppermute | solution.py:18
  159.6 21.8 %collective-permute-start.17 = (bf16[64,2560]{1,0:T(8,128)(2,1)S(1)}, bf16[64,2560]{1,0:T(8,128)(2,1)S(1)}, u32[]{:S(2)}, u32[]{:S(2)}) collective-permute-start(bf16[64,2560]{1,0:T(8,128)(2,1)S(1)} %fusion.13), channel_id=1, source_target_pairs={{0,8},{4,12},{8,0},{12,4},{1,9},{5,13},{9,1},{13,5},{2,10},{6,14},... | collective-permute-start | bytes 983048 | tf_op jit(solution)/shard_map/ppermute | solution.py:18
  173.2 85.2 %collective-permute-start.25 = (bf16[640,640]{1,0:T(8,128)(2,1)S(1)}, bf16[640,640]{1,0:T(8,128)(2,1)S(1)}, u32[]{:S(2)}, u32[]{:S(2)}) collective-permute-start(bf16[640,640]{1,0:T(8,128)(2,1)S(1)} %get-tuple-element.8), channel_id=1, source_target_pairs={{3,2},{2,1},{7,6},{6,5},{11,10},{10,9},{15,14},{14,13},{19,18},{18... | collective-permute-start | bytes 2457608 | tf_op jit(solution)/shard_map/ppermute | solution.py:76
  173.9 91.1 %collective-permute-start.23 = (bf16[640,640]{1,0:T(8,128)(2,1)}, bf16[640,640]{1,0:T(8,128)(2,1)}, u32[]{:S(2)}, u32[]{:S(2)}) collective-permute-start(bf16[640,640]{1,0:T(8,128)(2,1)} %get-tuple-element.7), channel_id=1, source_target_pairs={{0,1},{1,2},{2,3},{4,5},{5,6},{6,7},{8,9},{9,10},{10,11},{12,13},{... | collective-permute-start | bytes 2457608 | tf_op jit(solution)/shard_map/ppermute | solution.py:75
  187.7 75.0 %collective-permute-start.27 = (f32[128]{0:T(128)S(1)}, f32[128]{0:T(128)S(1)}, u32[]{:S(2)}, u32[]{:S(2)}) collective-permute-start(f32[128]{0:T(128)S(1)} %get-tuple-element.5), channel_id=1, source_target_pairs={{0,16},{16,0},{1,17},{17,1},{2,18},{18,2},{3,19},{19,3},{4,20},{20... | collective-permute-start | bytes 1544 | tf_op jit(solution)/shard_map/ppermute | solution.py:18
  259.6 17.6 %collective-permute-start.26 = (bf16[640,640]{1,0:T(8,128)(2,1)}, bf16[640,640]{1,0:T(8,128)(2,1)}, u32[]{:S(2)}, u32[]{:S(2)}) collective-permute-start(bf16[640,640]{1,0:T(8,128)(2,1)} %add_convert_fusion), channel_id=1, source_target_pairs={{3,2},{2,1},{1,0},{7,6},{6,5},{5,4},{11,10},{10,9},{9,8},{15,14},{... | collective-permute-start | bytes 2457608 | tf_op jit(solution)/shard_map/ppermute | solution.py:76
  (21 other events, 245.5 us)

commit v2 on v1

--- a/solution.py
+++ b/solution.py
@@ -163,20 +163,20 @@
     unit_half = own_half(hidden) * inverse_rms
     scaled = grad_half * gain_half
     inner_sum = jnp.sum(scaled * unit_half, axis=-1)
-    inner_sum = inner_sum + swap(inner_sum, "grp", 1)
+    tok_sums = jnp.concatenate([inner_sum, jnp.full((128,), squared, F32)])
+    tok_sums = tok_sums + swap(tok_sums, "grp", 1)
+    inner_sum = tok_sums[:tok_rows]
     mean_term = inner_sum[:, None] / D_S
     grad_hidden = inverse_rms * (scaled - unit_half * mean_term)
 
-    sums = jnp.concatenate(
-        [jnp.sum(grad_half * unit_half, axis=0), jnp.full((128,), squared, F32)]
-    )
-    gathered = lax.all_gather(sums, ("grp", "dp", "mp"), axis=0, tiled=False)
-    gathered = gathered.reshape(lax.axis_size("grp"), -1, width_half + 128)
-    grad_gain = (
-        jnp.sum(lax.dynamic_index_in_dim(gathered, grp, 0, False)[:, :width_half], axis=0)
-        / live_count
-    )
-    distill_loss = jnp.sum(gathered[:, :, width_half]) / (live_count * D_T)
+    sums = jnp.concatenate([jnp.sum(grad_half * unit_half, axis=0), tok_sums[tok_rows:]])
+    for axis in ("dp", "mp"):
+        flip = 1
+        while flip < lax.axis_size(axis):
+            sums = sums + swap(sums, axis, flip)
+            flip *= 2
+    grad_gain = sums[:width_half] / live_count
+    distill_loss = sums[width_half] / (live_count * D_T)
     return (own_target[None], distill_loss, grad_proj, grad_gain, grad_hidden[None])
 
 

time: 282 us -> 231 us (0.82)
  blocking collectives: 68.4 us -> 0 us
  waiting for transfers between devices: 64.8 us -> 74.7 us
  starting transfers between devices: 70.1 us -> 76.1 us
    all_gather x1 -> x0, blocking collectives: 68.4 us -> none  [body(): gathered = lax.all_gather(sums, ('grp', 'dp', 'mp'), axis=0, tiled=False)]
    ppermute x10 -> x14, waiting for transfers between devices: 9.92 us -> 28.1 us  [swap(): lax.ppermute(array, axis, [(i, i ^ flip) for i in range(lax.axis_size(axi...]
    ppermute x9, waiting for transfers between devices: 14.9 us -> 2.78 us  [line_scatter_sum(): downs[sub] = lax.ppermute(down, axis, down_pairs)]
    ppermute x10 -> x14, starting transfers between devices: 11.5 us -> 17.2 us  [swap(): lax.ppermute(array, axis, [(i, i ^ flip) for i in range(lax.axis_size(axi...]
    ppermute x9, waiting for transfers between devices: 40 us -> 43.9 us  [line_scatter_sum(): ups[sub] = lax.ppermute(up, axis, up_pairs)]
  transfers between devices with their start and end apart: 28 -> 32, of which waited for: 14 -> 17; matrix products, arithmetic and copies ran while one was open for 14% -> 17% of each run, Pallas kernels for 0% -> 0%
where the time goes in v2:
time: 231 us; the launch traced here: 230 us
  starting transfers between devices  76.1 us (33%)
  waiting for transfers between devices  74.7 us (32%)
  other arithmetic  35.7 us (15%)
  matrix products  19 us (8%)
  local copies, waits for them, and re-layouts  10.7 us (5%)
  Pallas kernels  9.7 us (4%)
  between operations  3.62 us (2%)
    ppermute x9, starting transfers between devices, line_scatter_sum(): ups[sub] = lax.ppermute(up, axis, up_pairs)  47 us
    ppermute x9, waiting for transfers between devices, line_scatter_sum(): ups[sub] = lax.ppermute(up, axis, up_pairs)  43.9 us
    ppermute x14, waiting for transfers between devices, swap(): lax.ppermute(array, axis, [(i, i ^ flip) for i in range(lax.axis_size(axi...  28.1 us
    ppermute x14, starting transfers between devices, swap(): lax.ppermute(array, axis, [(i, i ^ flip) for i in range(lax.axis_size(axi...  17.2 us
    ppermute x9, starting transfers between devices, line_scatter_sum(): downs[sub] = lax.ppermute(down, axis, down_pairs)  11.9 us
    pallas_call x1, Pallas kernels, attend(): pl.pallas_call(attend_kernel, grid=(width // HD, rows // block), in_specs...  9.7 us
    convert_element_type x5, other arithmetic, line_scatter_sum(): up = (up.astype(F32) + ups[sub].astype(F32)).astype(BF)  8.72 us
    dot_general x1, matrix products, body(): jnp.dot(context, weight_half, preferred_element_type=F32).astype(BF)  5.58 us
  transfers between devices with their start and end apart: 32, of which 17 were waited for; matrix products, arithmetic and copies ran while one was open for 17% of the time, Pallas kernels for 0%

profile of v2, /device:TPU:0, one launch (start us, length us, event | category | flops | bytes accessed | tf_op | source)
XLA Modules:
  0.0 229.6 jit_solution(8482903856228091287)
XLA Ops:
  3.1 9.7 %shard_map.128 = bf16[512,1024]{1,0:T(8,128)(2,1)S(1)} custom-call(bf16[512,1024]{1,0:T(8,128)(2,1)S(1)} %bitcast.55, bf16[512,128]{1,0:T(8,128)(2,1)S(1)} %get-tuple-element.36.k_ref, bf16[512,128]{1,0:T(8,128)(2,1)S(1)} %get-tuple-element.35.v_ref), custom_call_target="tpu_custom_call" | custom-call | flops 1073741824 | bytes 2359296 | tf_op jit(solution)/shard_map/pallas_call | solution.py:41
  12.8 5.6 %fusion.2 = bf16[512,2560]{1,0:T(8,128)(2,1)S(1)} fusion(bf16[512,1024]{1,0:T(8,128)(2,1)S(1)} %shard_map.128, bf16[1024,5120]{1,0:T(8,128)(2,1)} %param.12, s32[]{:T(128)S(6)} %select_n.109), kind=kOutput, calls=%fused_computation.3 | convolution fusion | flops 2685665280 | bytes 8912900 | tf_op jit(solution)/shard_map/dot_general | solution.py:108
  20.9 5.6 %collective-permute-start = (bf16[128,1280]{1,0:T(8,128)(2,1)}, bf16[128,1280]{1,0:T(8,128)(2,1)}, u32[]{:S(2)}, u32[]{:S(2)}) collective-permute-start(bf16[128,1280]{1,0:T(8,128)(2,1)} %get-tuple-element.16), channel_id=1, source_target_pairs={{0,1},{4,5},{8,9},{12,13},{16,17},{20,21},{24,25},{28,29}} | collective-permute-start | bytes 983048 | tf_op jit(solution)/shard_map/ppermute | solution.py:75
  28.0 5.2 %collective-permute-done = bf16[128,1280]{1,0:T(8,128)(2,1)} collective-permute-done((bf16[128,1280]{1,0:T(8,128)(2,1)}, bf16[128,1280]{1,0:T(8,128)(2,1)}, u32[]{:S(2)}, u32[]{:S(2)}) %collective-permute-start) | collective-permute-done | bytes 327712 | tf_op jit(solution)/shard_map/ppermute | solution.py:75
  35.0 5.1 %collective-permute-start.1 = (bf16[128,1280]{1,0:T(8,128)(2,1)}, bf16[128,1280]{1,0:T(8,128)(2,1)}, u32[]{:S(2)}, u32[]{:S(2)}) collective-permute-start(bf16[128,1280]{1,0:T(8,128)(2,1)} %add_convert_fusion.11), channel_id=1, source_target_pairs={{0,1},{1,2},{4,5},{5,6},{8,9},{9,10},{12,13},{13,14},{16,17},{17,1... | collective-permute-start | bytes 983048 | tf_op jit(solution)/shard_map/ppermute | solution.py:75
  40.1 5.7 %collective-permute-done.1 = bf16[128,1280]{1,0:T(8,128)(2,1)} collective-permute-done((bf16[128,1280]{1,0:T(8,128)(2,1)}, bf16[128,1280]{1,0:T(8,128)(2,1)}, u32[]{:S(2)}, u32[]{:S(2)}) %collective-permute-start.1) | collective-permute-done | bytes 327712 | tf_op jit(solution)/shard_map/ppermute | solution.py:75
  49.4 5.0 %collective-permute-start.6 = (bf16[128,1280]{1,0:T(8,128)(2,1)}, bf16[128,1280]{1,0:T(8,128)(2,1)}, u32[]{:S(2)}, u32[]{:S(2)}) collective-permute-start(bf16[128,1280]{1,0:T(8,128)(2,1)} %get-tuple-element.18), channel_id=1, source_target_pairs={{0,1},{4,5},{8,9},{12,13},{16,17},{20,21},{24,25},{28,29}} | collective-permute-start | bytes 983048 | tf_op jit(solution)/shard_map/ppermute | solution.py:75
  62.2 4.0 %collective-permute-done.2 = bf16[128,1280]{1,0:T(8,128)(2,1)S(1)} collective-permute-done((bf16[128,1280]{1,0:T(8,128)(2,1)}, bf16[128,1280]{1,0:T(8,128)(2,1)S(1)}, u32[]{:S(2)}, u32[]{:S(2)}) %collective-permute-start.2) | collective-permute-done | bytes 327712 | tf_op jit(solution)/shard_map/ppermute | solution.py:75
  68.5 2.6 %convert_add_fusion.4 = (f32[128,1280]{1,0:T(8,128)}, bf16[128,1280]{1,0:T(8,128)(2,1)}, bf16[128,1280]{1,0:T(8,128)(2,1)}) fusion(bf16[128,1280]{1,0:T(8,128)(2,1)S(1)} %collective-permute-done.5, bf16[128,1280]{1,0:T(8,128)(2,1)S(1)} %collective-permute-done.2, bf16[512,2560]{1,0:T(8,128)(2,1)} %copy-done.4, s32[]{:T(128)S(6)} %select_n.112, ...), kind=kLoop, calls=%fused_computation.45 | loop fusion | flops 2129920 | bytes 3604492 | tf_op jit(solution)/shard_map/add | solution.py:78
  72.4 5.6 %collective-permute-start.7 = (bf16[128,1280]{1,0:T(8,128)(2,1)}, bf16[128,1280]{1,0:T(8,128)(2,1)}, u32[]{:S(2)}, u32[]{:S(2)}) collective-permute-start(bf16[128,1280]{1,0:T(8,128)(2,1)} %get-tuple-element.13), channel_id=1, source_target_pairs={{0,1},{1,2},{4,5},{5,6},{8,9},{9,10},{12,13},{13,14},{16,17},{17,1... | collective-permute-start | bytes 983048 | tf_op jit(solution)/shard_map/ppermute | solution.py:75
  84.9 6.9 %collective-permute-start.8 = (bf16[128,1280]{1,0:T(8,128)(2,1)S(1)}, bf16[128,1280]{1,0:T(8,128)(2,1)S(1)}, u32[]{:S(2)}, u32[]{:S(2)}) collective-permute-start(bf16[128,1280]{1,0:T(8,128)(2,1)S(1)} %get-tuple-element.20), channel_id=1, source_target_pairs={{0,1},{1,2},{2,3},{4,5},{5,6},{6,7},{8,9},{9,10},{10,11},{12,13},{... | collective-permute-start | bytes 983048 | tf_op jit(solution)/shard_map/ppermute | solution.py:75
  100.8 6.1 %collective-permute-done.14 = bf16[128,1280]{1,0:T(8,128)(2,1)} collective-permute-done((bf16[128,1280]{1,0:T(8,128)(2,1)}, bf16[128,1280]{1,0:T(8,128)(2,1)}, u32[]{:S(2)}, u32[]{:S(2)}) %collective-permute-start.14) | collective-permute-done | bytes 327712 | tf_op jit(solution)/shard_map/ppermute | solution.py:18
  110.9 4.6 %multiply_reduce_fusion = (f32[]{:T(128)}, bf16[512,640]{1,0:T(8,128)(2,1)S(1)}) fusion(bf16[256,640]{1,0:T(8,128)(2,1)S(1)} %collective-permute-done.15, bf16[256,640]{1,0:T(8,128)(2,1)S(1)} %get-tuple-element.24, bf16[2560,640]{1,0:T(8,128)(2,1)S(1)} %copy-done, bf16[256,2560]{1,0:T(8,128)(2,1)} %collective-permute-done.13, ...), kind=kOutput, calls=%fused_computation.25 | convolution fusion | flops 1688535040 | bytes 7209476 | tf_op jit(solution)/shard_map/dot_general | solution.py:121
  118.3 3.9 %convolution_convert_fusion = bf16[2560,640]{1,0:T(8,128)(2,1)S(1)} fusion(bf16[512,640]{1,0:T(8,128)(2,1)S(1)} %get-tuple-element.23, bf16[256,2560]{1,0:T(8,128)(2,1)} %collective-permute-done.13, bf16[128,2560]{1,0:T(8,128)(2,1)} %collective-permute-done.12, bf16[128,2560]{1,0:T(8,128)(2,1)} %fusion.11), kind=kOutput, calls=%fused_computation.2 | convolution fusion | flops 1687224320 | bytes 6553600 | tf_op jit(solution)/shard_map/dot_general | solution.py:157
  124.4 7.7 %collective-permute-start.26 = (bf16[640,640]{1,0:T(8,128)(2,1)}, bf16[640,640]{1,0:T(8,128)(2,1)}, u32[]{:S(2)}, u32[]{:S(2)}) collective-permute-start(bf16[640,640]{1,0:T(8,128)(2,1)} %get-tuple-element.9), channel_id=1, source_target_pairs={{0,1},{4,5},{8,9},{12,13},{16,17},{20,21},{24,25},{28,29}} | collective-permute-start | bytes 2457608 | tf_op jit(solution)/shard_map/ppermute | solution.py:75
  135.3 13.9 %collective-permute-done.26 = bf16[640,640]{1,0:T(8,128)(2,1)} collective-permute-done((bf16[640,640]{1,0:T(8,128)(2,1)}, bf16[640,640]{1,0:T(8,128)(2,1)}, u32[]{:S(2)}, u32[]{:S(2)}) %collective-permute-start.26) | collective-permute-done | bytes 819232 | tf_op jit(solution)/shard_map/ppermute | solution.py:75
  150.8 4.6 %collective-permute-start.27 = (bf16[640,640]{1,0:T(8,128)(2,1)S(1)}, bf16[640,640]{1,0:T(8,128)(2,1)S(1)}, u32[]{:S(2)}, u32[]{:S(2)}) collective-permute-start(bf16[640,640]{1,0:T(8,128)(2,1)S(1)} %add_convert_fusion.3), channel_id=1, source_target_pairs={{0,1},{1,2},{4,5},{5,6},{8,9},{9,10},{12,13},{13,14},{16,17},{17,1... | collective-permute-start | bytes 2457608 | tf_op jit(solution)/shard_map/ppermute | solution.py:75
  161.3 10.7 %collective-permute-done.27 = bf16[640,640]{1,0:T(8,128)(2,1)S(1)} collective-permute-done((bf16[640,640]{1,0:T(8,128)(2,1)S(1)}, bf16[640,640]{1,0:T(8,128)(2,1)S(1)}, u32[]{:S(2)}, u32[]{:S(2)}) %collective-permute-start.27) | collective-permute-done | bytes 819232 | tf_op jit(solution)/shard_map/ppermute | solution.py:75
  184.4 3.0 %collective-permute-done.21 = f32[256]{0:T(256)S(1)} collective-permute-done((f32[256]{0:T(256)S(1)}, f32[256]{0:T(256)S(1)}, u32[]{:S(2)}, u32[]{:S(2)}) %collective-permute-start.21) | collective-permute-done | bytes 1056 | tf_op jit(solution)/shard_map/ppermute | solution.py:18
  192.2 5.2 %collective-permute-start.28 = (bf16[640,640]{1,0:T(8,128)(2,1)}, bf16[640,640]{1,0:T(8,128)(2,1)}, u32[]{:S(2)}, u32[]{:S(2)}) collective-permute-start(bf16[640,640]{1,0:T(8,128)(2,1)} %get-tuple-element.7), channel_id=1, source_target_pairs={{0,1},{1,2},{2,3},{4,5},{5,6},{6,7},{8,9},{9,10},{10,11},{12,13},{... | collective-permute-start | bytes 2457608 | tf_op jit(solution)/shard_map/ppermute | solution.py:75
  205.2 9.1 %collective-permute-done.24 = f32[1408]{0:T(1024)S(1)} collective-permute-done((f32[1408]{0:T(1024)S(1)}, f32[1408]{0:T(1024)S(1)}, u32[]{:S(2)}, u32[]{:S(2)}) %collective-permute-start.24) | collective-permute-done | bytes 5664 | tf_op jit(solution)/shard_map/ppermute | solution.py:18
  214.4 3.2 %collective-permute-start.25 = (f32[1408]{0:T(1024)S(1)}, f32[1408]{0:T(1024)S(1)}, u32[]{:S(2)}, u32[]{:S(2)}) collective-permute-start(f32[1408]{0:T(1024)S(1)} %add.342), channel_id=1, source_target_pairs={{0,2},{1,3},{2,0},{3,1},{4,6},{5,7},{6,4},{7,5},{8,10},{9,11},{10,... | collective-permute-start | bytes 16904 | tf_op jit(solution)/shard_map/ppermute | solution.py:18
  218.7 4.9 %collective-permute-done.25 = f32[1408]{0:T(1024)S(1)} collective-permute-done((f32[1408]{0:T(1024)S(1)}, f32[1408]{0:T(1024)S(1)}, u32[]{:S(2)}, u32[]{:S(2)}) %collective-permute-start.25) | collective-permute-done | bytes 5664 | tf_op jit(solution)/shard_map/ppermute | solution.py:18
  225.3 3.1 %add_divide_fusion = f32[640,640]{1,0:T(8,128)} fusion(bf16[640,640]{1,0:T(8,128)(2,1)} %collective-permute-done.31, bf16[640,640]{1,0:T(8,128)(2,1)} %collective-permute-done.28, f32[]{:T(128)S(6)} %convert_element_type.257, bf16[2560,640]{1,0:T(8,128)(2,1)} %copy-done.2, s32[]{:T(128)S(6)} %select_n.132), kind=kLoop, calls=%fused_computation.7 | loop fusion | flops 2457600 | bytes 4096008 | tf_op jit(solution)/shard_map/div | solution.py:160
  (137 shorter events, 84.9 us)
Async XLA Ops:
  20.9 12.2 %collective-permute-start = (bf16[128,1280]{1,0:T(8,128)(2,1)}, bf16[128,1280]{1,0:T(8,128)(2,1)}, u32[]{:S(2)}, u32[]{:S(2)}) collective-permute-start(bf16[128,1280]{1,0:T(8,128)(2,1)} %get-tuple-element.16), channel_id=1, source_target_pairs={{0,1},{4,5},{8,9},{12,13},{16,17},{20,21},{24,25},{28,29}} | collective-permute-start | bytes 983048 | tf_op jit(solution)/shard_map/ppermute | solution.py:75
  26.6 13.5 %collective-permute-start.3 = (bf16[128,1280]{1,0:T(8,128)(2,1)}, bf16[128,1280]{1,0:T(8,128)(2,1)}, u32[]{:S(2)}, u32[]{:S(2)}) collective-permute-start(bf16[128,1280]{1,0:T(8,128)(2,1)} %get-tuple-element.19), channel_id=1, source_target_pairs={{3,2},{7,6},{11,10},{15,14},{19,18},{23,22},{27,26},{31,30}} | collective-permute-start | bytes 983048 | tf_op jit(solution)/shard_map/ppermute | solution.py:76
  35.0 10.8 %collective-permute-start.1 = (bf16[128,1280]{1,0:T(8,128)(2,1)}, bf16[128,1280]{1,0:T(8,128)(2,1)}, u32[]{:S(2)}, u32[]{:S(2)}) collective-permute-start(bf16[128,1280]{1,0:T(8,128)(2,1)} %add_convert_fusion.11), channel_id=1, source_target_pairs={{0,1},{1,2},{4,5},{5,6},{8,9},{9,10},{12,13},{13,14},{16,17},{17,1... | collective-permute-start | bytes 983048 | tf_op jit(solution)/shard_map/ppermute | solution.py:75
  48.0 9.1 %collective-permute-start.4 = (bf16[128,1280]{1,0:T(8,128)(2,1)}, bf16[128,1280]{1,0:T(8,128)(2,1)}, u32[]{:S(2)}, u32[]{:S(2)}) collective-permute-start(bf16[128,1280]{1,0:T(8,128)(2,1)} %get-tuple-element.15), channel_id=1, source_target_pairs={{3,2},{2,1},{7,6},{6,5},{11,10},{10,9},{15,14},{14,13},{19,18},{18... | collective-permute-start | bytes 983048 | tf_op jit(solution)/shard_map/ppermute | solution.py:76
  49.4 12.8 %collective-permute-start.6 = (bf16[128,1280]{1,0:T(8,128)(2,1)}, bf16[128,1280]{1,0:T(8,128)(2,1)}, u32[]{:S(2)}, u32[]{:S(2)}) collective-permute-start(bf16[128,1280]{1,0:T(8,128)(2,1)} %get-tuple-element.18), channel_id=1, source_target_pairs={{0,1},{4,5},{8,9},{12,13},{16,17},{20,21},{24,25},{28,29}} | collective-permute-start | bytes 983048 | tf_op jit(solution)/shard_map/ppermute | solution.py:75
  55.8 10.4 %collective-permute-start.2 = (bf16[128,1280]{1,0:T(8,128)(2,1)}, bf16[128,1280]{1,0:T(8,128)(2,1)S(1)}, u32[]{:S(2)}, u32[]{:S(2)}) collective-permute-start(bf16[128,1280]{1,0:T(8,128)(2,1)} %get-tuple-element.14), channel_id=1, source_target_pairs={{0,1},{1,2},{2,3},{4,5},{5,6},{6,7},{8,9},{9,10},{10,11},{12,13},{... | collective-permute-start | bytes 983048 | tf_op jit(solution)/shard_map/ppermute | solution.py:75
  58.3 10.2 %collective-permute-start.5 = (bf16[128,1280]{1,0:T(8,128)(2,1)S(1)}, bf16[128,1280]{1,0:T(8,128)(2,1)S(1)}, u32[]{:S(2)}, u32[]{:S(2)}) collective-permute-start(bf16[128,1280]{1,0:T(8,128)(2,1)S(1)} %add_convert_fusion.8), channel_id=1, source_target_pairs={{3,2},{2,1},{1,0},{7,6},{6,5},{5,4},{11,10},{10,9},{9,8},{15,14},{... | collective-permute-start | bytes 983048 | tf_op jit(solution)/shard_map/ppermute | solution.py:76
  71.1 9.6 %collective-permute-start.10 = (bf16[128,1280]{1,0:T(8,128)(2,1)}, bf16[128,1280]{1,0:T(8,128)(2,1)}, u32[]{:S(2)}, u32[]{:S(2)}) collective-permute-start(bf16[128,1280]{1,0:T(8,128)(2,1)} %get-tuple-element.12), channel_id=1, source_target_pairs={{3,2},{2,1},{7,6},{6,5},{11,10},{10,9},{15,14},{14,13},{19,18},{18... | collective-permute-start | bytes 983048 | tf_op jit(solution)/shard_map/ppermute | solution.py:76
  72.4 9.7 %collective-permute-start.7 = (bf16[128,1280]{1,0:T(8,128)(2,1)}, bf16[128,1280]{1,0:T(8,128)(2,1)}, u32[]{:S(2)}, u32[]{:S(2)}) collective-permute-start(bf16[128,1280]{1,0:T(8,128)(2,1)} %get-tuple-element.13), channel_id=1, source_target_pairs={{0,1},{1,2},{4,5},{5,6},{8,9},{9,10},{12,13},{13,14},{16,17},{17,1... | collective-permute-start | bytes 983048 | tf_op jit(solution)/shard_map/ppermute | solution.py:75
  79.1 12.7 %collective-permute-start.12 = (bf16[128,2560]{1,0:T(8,128)(2,1)}, bf16[128,2560]{1,0:T(8,128)(2,1)}, u32[]{:S(2)}, u32[]{:S(2)}) collective-permute-start(bf16[128,2560]{1,0:T(8,128)(2,1)} %fusion.11), channel_id=1, source_target_pairs={{0,8},{4,12},{8,0},{12,4},{1,9},{5,13},{9,1},{13,5},{2,10},{6,14},... | collective-permute-start | bytes 1966088 | tf_op jit(solution)/shard_map/ppermute | solution.py:18
  83.6 11.1 %collective-permute-start.11 = (bf16[128,1280]{1,0:T(8,128)(2,1)S(1)}, bf16[128,1280]{1,0:T(8,128)(2,1)S(1)}, u32[]{:S(2)}, u32[]{:S(2)}) collective-permute-start(bf16[128,1280]{1,0:T(8,128)(2,1)S(1)} %get-tuple-element.21), channel_id=1, source_target_pairs={{3,2},{2,1},{1,0},{7,6},{6,5},{5,4},{11,10},{10,9},{9,8},{15,14},{... | collective-permute-start | bytes 983048 | tf_op jit(solution)/shard_map/ppermute | solution.py:76
  84.9 11.4 %collective-permute-start.8 = (bf16[128,1280]{1,0:T(8,128)(2,1)S(1)}, bf16[128,1280]{1,0:T(8,128)(2,1)S(1)}, u32[]{:S(2)}, u32[]{:S(2)}) collective-permute-start(bf16[128,1280]{1,0:T(8,128)(2,1)S(1)} %get-tuple-element.20), channel_id=1, source_target_pairs={{0,1},{1,2},{2,3},{4,5},{5,6},{6,7},{8,9},{9,10},{10,11},{12,13},{... | collective-permute-start | bytes 983048 | tf_op jit(solution)/shard_map/ppermute | solution.py:75
  94.3 16.6 %collective-permute-start.13 = (bf16[256,2560]{1,0:T(8,128)(2,1)}, bf16[256,2560]{1,0:T(8,128)(2,1)}, u32[]{:S(2)}, u32[]{:S(2)}) collective-permute-start(bf16[256,2560]{1,0:T(8,128)(2,1)} %pad_maximum_fusion.1), channel_id=1, source_target_pairs={{0,4},{4,0},{8,12},{12,8},{1,5},{5,1},{9,13},{13,9},{2,6},{6,2},{1... | collective-permute-start | bytes 3932168 | tf_op jit(solution)/shard_map/ppermute | solution.py:18
  117.8 37.6 %collective-permute-start.16 = (bf16[256,2560]{1,0:T(8,128)(2,1)}, bf16[256,2560]{1,0:T(8,128)(2,1)}, u32[]{:S(2)}, u32[]{:S(2)}) collective-permute-start(bf16[256,2560]{1,0:T(8,128)(2,1)} %convolution_convert_fusion.1), channel_id=1, source_target_pairs={{0,4},{4,0},{8,12},{12,8},{1,5},{5,1},{9,13},{13,9},{2,6},{6,2},{1... | collective-permute-start | bytes 3932168 | tf_op jit(solution)/shard_map/ppermute | solution.py:18
  124.4 24.8 %collective-permute-start.26 = (bf16[640,640]{1,0:T(8,128)(2,1)}, bf16[640,640]{1,0:T(8,128)(2,1)}, u32[]{:S(2)}, u32[]{:S(2)}) collective-permute-start(bf16[640,640]{1,0:T(8,128)(2,1)} %get-tuple-element.9), channel_id=1, source_target_pairs={{0,1},{4,5},{8,9},{12,13},{16,17},{20,21},{24,25},{28,29}} | collective-permute-start | bytes 2457608 | tf_op jit(solution)/shard_map/ppermute | solution.py:75
  134.5 26.9 %collective-permute-start.29 = (bf16[640,640]{1,0:T(8,128)(2,1)}, bf16[640,640]{1,0:T(8,128)(2,1)S(1)}, u32[]{:S(2)}, u32[]{:S(2)}) collective-permute-start(bf16[640,640]{1,0:T(8,128)(2,1)} %get-tuple-element.10), channel_id=1, source_target_pairs={{3,2},{7,6},{11,10},{15,14},{19,18},{23,22},{27,26},{31,30}} | collective-permute-start | bytes 2457608 | tf_op jit(solution)/shard_map/ppermute | solution.py:76
  150.8 21.2 %collective-permute-start.27 = (bf16[640,640]{1,0:T(8,128)(2,1)S(1)}, bf16[640,640]{1,0:T(8,128)(2,1)S(1)}, u32[]{:S(2)}, u32[]{:S(2)}) collective-permute-start(bf16[640,640]{1,0:T(8,128)(2,1)S(1)} %add_convert_fusion.3), channel_id=1, source_target_pairs={{0,1},{1,2},{4,5},{5,6},{8,9},{9,10},{12,13},{13,14},{16,17},{17,1... | collective-permute-start | bytes 2457608 | tf_op jit(solution)/shard_map/ppermute | solution.py:75
  158.2 17.0 %collective-permute-start.17 = (bf16[64,2560]{1,0:T(8,128)(2,1)S(1)}, bf16[64,2560]{1,0:T(8,128)(2,1)S(1)}, u32[]{:S(2)}, u32[]{:S(2)}) collective-permute-start(bf16[64,2560]{1,0:T(8,128)(2,1)S(1)} %fusion.13), channel_id=1, source_target_pairs={{0,8},{4,12},{8,0},{12,4},{1,9},{5,13},{9,1},{13,5},{2,10},{6,14},... | collective-permute-start | bytes 983048 | tf_op jit(solution)/shard_map/ppermute | solution.py:18
  159.8 17.0 %collective-permute-start.19 = (bf16[2,64,1280]{2,1,0:T(8,128)(2,1)S(1)}, bf16[2,64,1280]{2,1,0:T(8,128)(2,1)S(1)}, u32[]{:S(2)}, u32[]{:S(2)}) collective-permute-start(bf16[2,64,1280]{2,1,0:T(8,128)(2,1)S(1)} %dynamic-slice_convert_fusion), channel_id=1, source_target_pairs={{0,16},{16,0},{1,17},{17,1},{2,18},{18,2},{3,19},{19,3},{4,20},{20... | collective-permute-start | bytes 983048 | tf_op jit(solution)/shard_map/ppermute | solution.py:18
  173.6 25.6 %collective-permute-start.30 = (bf16[640,640]{1,0:T(8,128)(2,1)}, bf16[640,640]{1,0:T(8,128)(2,1)}, u32[]{:S(2)}, u32[]{:S(2)}) collective-permute-start(bf16[640,640]{1,0:T(8,128)(2,1)} %get-tuple-element.8), channel_id=1, source_target_pairs={{3,2},{2,1},{7,6},{6,5},{11,10},{10,9},{15,14},{14,13},{19,18},{18... | collective-permute-start | bytes 2457608 | tf_op jit(solution)/shard_map/ppermute | solution.py:76
  192.2 33.2 %collective-permute-start.28 = (bf16[640,640]{1,0:T(8,128)(2,1)}, bf16[640,640]{1,0:T(8,128)(2,1)}, u32[]{:S(2)}, u32[]{:S(2)}) collective-permute-start(bf16[640,640]{1,0:T(8,128)(2,1)} %get-tuple-element.7), channel_id=1, source_target_pairs={{0,1},{1,2},{2,3},{4,5},{5,6},{6,7},{8,9},{9,10},{10,11},{12,13},{... | collective-permute-start | bytes 2457608 | tf_op jit(solution)/shard_map/ppermute | solution.py:75
  197.4 17.0 %collective-permute-start.24 = (f32[1408]{0:T(1024)S(1)}, f32[1408]{0:T(1024)S(1)}, u32[]{:S(2)}, u32[]{:S(2)}) collective-permute-start(f32[1408]{0:T(1024)S(1)} %add.341), channel_id=1, source_target_pairs={{0,1},{1,0},{2,3},{3,2},{4,5},{5,4},{6,7},{7,6},{8,9},{9,8},{10,11... | collective-permute-start | bytes 16904 | tf_op jit(solution)/shard_map/ppermute | solution.py:18
  201.7 23.6 %collective-permute-start.31 = (bf16[640,640]{1,0:T(8,128)(2,1)}, bf16[640,640]{1,0:T(8,128)(2,1)}, u32[]{:S(2)}, u32[]{:S(2)}) collective-permute-start(bf16[640,640]{1,0:T(8,128)(2,1)} %add_convert_fusion), channel_id=1, source_target_pairs={{3,2},{2,1},{1,0},{7,6},{6,5},{5,4},{11,10},{10,9},{9,8},{15,14},{... | collective-permute-start | bytes 2457608 | tf_op jit(solution)/shard_map/ppermute | solution.py:76
  214.4 9.2 %collective-permute-start.25 = (f32[1408]{0:T(1024)S(1)}, f32[1408]{0:T(1024)S(1)}, u32[]{:S(2)}, u32[]{:S(2)}) collective-permute-start(f32[1408]{0:T(1024)S(1)} %add.342), channel_id=1, source_target_pairs={{0,2},{1,3},{2,0},{3,1},{4,6},{5,7},{6,4},{7,5},{8,10},{9,11},{10,... | collective-permute-start | bytes 16904 | tf_op jit(solution)/shard_map/ppermute | solution.py:18
  (29 other events, 338.6 us)
